TPU v7x, 256 devices: a whole 4x4x8 slice. The times are simulated.
256 devices in a mesh: seq: 32 (over y, z), head: 8 (over x, core).
Axes of the slice: x: 4, y: 4, z: 8, core: 2. Of those that a mesh axis runs over, the one named last changes fastest.
Arguments:
- queries: bfloat16 [32768, 32, 128], P('seq', 'head'), may hold values from -6 to 6
- key_rows: bfloat16 [32768, 32, 128], P('seq', 'head'), may hold values from -6 to 6
- value_rows: bfloat16 [32768, 32, 128], P('seq', 'head'), may hold values from -6 to 6
- out_grad: bfloat16 [32768, 4096], P('seq', 'head'), may hold values from -6 to 6
- out_weight: bfloat16 [32, 128, 4096], P('head'), may hold values from -0.09375 to 0.09375
Outputs:
- query_grad: bfloat16 [32768, 32, 128], P('seq', 'head')
- key_grad: bfloat16 [32768, 32, 128], P('seq', 'head')
- value_grad: bfloat16 [32768, 32, 128], P('seq', 'head')
All inputs are finite; a program needn't handle non-finite values.
Results may differ from a plain program's by a relative error of at most 0.0058.
Values may be sent and summed in bfloat16 or wider, within the bound.
No kernel may reach another device: no remote copies, remote signals or barrier semaphores. Data moves between devices by JAX's collectives and lax.ppermute only.
A program may use at most 128 MiB of HBM per device.

v0:
```python
import math
import jax
import jax.numpy as jnp
from jax import lax
from jax.sharding import PartitionSpec as P

BLOCK = 256


def body(queries, key_rows, value_rows, out_grad, out_weight):
    tokens = queries.shape[0]
    heads = queries.shape[1]
    depth = queries.shape[2]
    blocks = tokens // BLOCK
    factor = 1.0 / math.sqrt(depth * tokens * lax.axis_size("seq"))
    attn_grad = jnp.einsum(
        "tm,hdm->thd",
        lax.all_gather(out_grad, "head", axis=1, tiled=True),
        out_weight,
        preferred_element_type=jnp.float32,
    ).astype(jnp.bfloat16)
    layout = (blocks, BLOCK, heads, depth)
    query_blocks = queries.reshape(layout)
    key_blocks = key_rows.reshape(layout)
    value_blocks = value_rows.reshape(layout)
    grad_blocks = attn_grad.reshape(layout)
    kv_parts = jnp.einsum(
        "bthd,bthe->bhde", key_blocks, value_blocks, preferred_element_type=jnp.float32
    )
    qg_parts = jnp.einsum(
        "bthd,bthe->bhde", query_blocks, grad_blocks, preferred_element_type=jnp.float32
    )
    kv_total = jnp.sum(kv_parts, 0)
    qg_total = jnp.sum(qg_parts, 0)
    shards = lax.axis_size("seq")
    stacked = jnp.stack([kv_total, qg_total]).reshape(2, shards, -1)
    pieces = lax.all_to_all(stacked, "seq", split_axis=1, concat_axis=1, tiled=True)
    forward_sums = jnp.cumsum(pieces[0], 0) - pieces[0]
    reverse_sums = jnp.cumsum(pieces[1][::-1], 0)[::-1] - pieces[1]
    totals = lax.all_to_all(
        jnp.stack([forward_sums, reverse_sums]), "seq", split_axis=1, concat_axis=1, tiled=True
    )
    totals = totals.reshape(2, heads, depth, depth)
    before = totals[0]
    after = totals[1]
    first_zero = jnp.zeros((1, heads, depth, depth), jnp.float32)
    running = jnp.cumsum(kv_parts, 0)
    prefix = before[None] + jnp.concatenate([first_zero, running[:-1]], 0)
    backward_sums = jnp.cumsum(qg_parts[::-1], 0)[::-1]
    suffix = after[None] + jnp.concatenate([backward_sums[1:], first_zero], 0)
    prefix_bf = prefix.astype(jnp.bfloat16)
    suffix_bf = suffix.astype(jnp.bfloat16)
    causal = jnp.tril(jnp.ones((BLOCK, BLOCK), bool))
    qk_scores = jnp.einsum(
        "bthd,bshd->bhts", query_blocks, key_blocks, preferred_element_type=jnp.float32
    )
    qk_scores = jnp.where(causal, qk_scores, 0.0).astype(jnp.bfloat16)
    grad_scores = jnp.einsum(
        "bthd,bshd->bhts", grad_blocks, value_blocks, preferred_element_type=jnp.float32
    )
    grad_scores = jnp.where(causal, grad_scores, 0.0).astype(jnp.bfloat16)
    query_grad = jnp.einsum(
        "bhts,bshd->bthd", grad_scores, key_blocks, preferred_element_type=jnp.float32
    )
    query_grad = query_grad + jnp.einsum(
        "bthe,bhde->bthd", grad_blocks, prefix_bf, preferred_element_type=jnp.float32
    )
    key_grad = jnp.einsum(
        "bhts,bthd->bshd", grad_scores, query_blocks, preferred_element_type=jnp.float32
    )
    key_grad = key_grad + jnp.einsum(
        "bshe,bhde->bshd", value_blocks, suffix_bf, preferred_element_type=jnp.float32
    )
    value_grad = jnp.einsum(
        "bhts,bthe->bshe", qk_scores, grad_blocks, preferred_element_type=jnp.float32
    )
    value_grad = value_grad + jnp.einsum(
        "bshd,bhde->bshe", key_blocks, suffix_bf, preferred_element_type=jnp.float32
    )
    final_shape = (tokens, heads, depth)
    return (
        (factor * query_grad).astype(jnp.bfloat16).reshape(final_shape),
        (factor * key_grad).astype(jnp.bfloat16).reshape(final_shape),
        (factor * value_grad).astype(jnp.bfloat16).reshape(final_shape),
    )


def solution(mesh):
    placed = (
        P("seq", "head", None),
        P("seq", "head", None),
        P("seq", "head", None),
        P("seq", "head"),
        P("head", None, None),
    )
    return jax.shard_map(
        body,
        mesh=mesh,
        in_specs=placed,
        out_specs=(P("seq", "head", None), P("seq", "head", None), P("seq", "head", None)),
        check_vma=False,
    )
```

profile of v0, /device:TPU:32, one launch (start us, length us, event | category | flops | bytes accessed | tf_op | source)
XLA Modules:
  0.0 155.0 jit_solution(7390798430991049583)
XLA Ops:
  7.9 2.1 %fusion.38 = (f32[4,128,128]{2,1,0:T(8,128)S(1)}, f32[4,4,128,128]{3,2,1,0:T(8,128)S(1)}) fusion(bf16[4,256,4,128]{3,2,1,0:T(4,128)(2,1)} %bitcast.53, bf16[4,256,4,128]{3,2,1,0:T(4,128)(2,1)} %bitcast.46), kind=kOutput, calls=%fused_computation.48 | convolution fusion | flops 134414336 | bytes 3407872 | tf_op jit(solution)/shard_map/bthd,bthe->bhde/dot_general | solution.py:27
  10.0 54.7 %all-gather.2.cloned.1.call-done = bf16[1024,4096]{1,0:T(8,128)(2,1)} async-done(((bf16[1024,512]{1,0:T(8,128)(2,1)}), bf16[1024,4096]{1,0:T(8,128)(2,1)}) %all-gather.2.cloned.1.call-update) | async-done | bytes 8388624 | tf_op jit(solution)/shard_map/all_gather | solution.py:18
  64.7 8.2 %fusion.7 = bf16[1024,4,128]{2,0,1:T(8,128)(2,1)S(1)} fusion(bf16[4,128,4096]{2,1,0:T(8,128)(2,1)} %param.9, bf16[1024,4096]{1,0:T(8,128)(2,1)} %all-gather.2.cloned.1.call-done), kind=kOutput, calls=%fused_computation.12 | convolution fusion | flops 4295491584 | bytes 13631488 | tf_op jit(solution)/shard_map/tm,hdm->thd/dot_general | solution.py:16
  73.0 1.2 fusion.37
  74.2 1.1 copy.83
  75.4 1.2 copy.84
  76.6 10.1 %all-to-all-start = ((f32[2,32,2048]{2,0,1:T(2,128)}), f32[2,32,2048]{2,0,1:T(2,128)}, u32[]{:S(2)}, u32[]{:S(2)}) async-start(f32[2,32,2048]{2,0,1:T(2,128)} %copy.84), calls=%async_computation | async-start | bytes 1048576 | tf_op jit(solution)/shard_map/all_to_all | solution.py:37
  87.6 1.0 copy-done.9
  89.5 0.9 slice.31
  90.9 1.9 %select_convert_fusion.1 = bf16[4,4,256,256]{3,2,1,0:T(8,128)(2,1)S(1)} fusion(pred[256,256]{1,0:T(8,128)(4,1)S(1)} %iota_compare_fusion, bf16[4,256,4,128]{3,2,1,0:T(4,128)(2,1)S(1)} %bitcast.54, bf16[4,256,4,128]{3,1,0,2:T(8,128)(2,1)} %bitcast.57), kind=kOutput, calls=%fused_computation.3 | convolution fusion | flops 270532608 | bytes 4259840 | tf_op jit(solution)/shard_map/bthd,bshd->bhts/dot_general | solution.py:58
  92.9 12.0 %all-to-all-done = f32[2,32,2048]{2,0,1:T(2,128)} async-done(((f32[2,32,2048]{2,0,1:T(2,128)}), f32[2,32,2048]{2,0,1:T(2,128)}, u32[]{:S(2)}, u32[]{:S(2)}) %all-to-all-start) | async-done | bytes 524320 | tf_op jit(solution)/shard_map/all_to_all | solution.py:37
  104.9 1.7 %fusion.36 = (f32[1,32,2048]{2,0,1:T(1,128)S(1)}, f32[1,32,2048]{2,0,1:T(1,128)S(1)}) fusion(f32[2,32,2048]{2,0,1:T(2,128)} %all-to-all-done), kind=kLoop, calls=%fused_computation.46 | loop fusion | bytes 1048576 | tf_op jit(solution)/shard_map/slice | solution.py:38
  108.1 1.2 copy.87
  109.3 4.9 %all-to-all-start.1 = ((f32[2,32,2048]{2,0,1:T(2,128)}), f32[2,32,2048]{2,0,1:T(2,128)}, u32[]{:S(2)}, u32[]{:S(2)}) async-start(f32[2,32,2048]{2,0,1:T(2,128)} %copy.87), calls=%async_computation.1 | async-start | bytes 1048576 | tf_op jit(solution)/shard_map/all_to_all | solution.py:40
  114.2 3.4 %fusion.13 = f32[4,4,256,128]{3,2,1,0:T(8,128)} fusion(bf16[4,4,256,256]{3,2,1,0:T(8,128)(2,1)S(1)} %select_convert_fusion.1, bf16[4,256,4,128]{3,2,1,0:T(4,128)(2,1)} %bitcast.50), kind=kOutput, calls=%fused_computation.18 | convolution fusion | flops 268435456 | bytes 5242880 | tf_op jit(solution)/shard_map/bhts,bthd->bshd/dot_general | solution.py:68
  117.6 2.0 %fusion.24 = f32[4,4,256,128]{3,2,1,0:T(8,128)} fusion(bf16[4,4,256,256]{3,2,1,0:T(8,128)(2,1)S(1)} %select_convert_fusion.1, bf16[4,256,4,128]{3,2,1,0:T(4,128)(2,1)S(1)} %bitcast.47), kind=kOutput, calls=%fused_computation.28 | convolution fusion | flops 268435456 | bytes 5242880 | tf_op jit(solution)/shard_map/bhts,bshd->bthd/dot_general | solution.py:62
  119.7 3.9 %fusion.6 = f32[4,4,128,256]{3,2,1,0:T(8,128)} fusion(pred[256,256]{1,0:T(8,128)(4,1)S(1)} %iota_compare_fusion, bf16[4,256,4,128]{3,2,1,0:T(4,128)(2,1)} %bitcast.51, bf16[4,256,4,128]{3,2,1,0:T(4,128)(2,1)S(1)} %bitcast.48, bf16[4,256,4,128]{3,1,0,2:T(8,128)(2,1)} %bitcast.58), kind=kOutput, calls=%fused_computation.11 | convolution fusion | flops 538968064 | bytes 5308416 | tf_op jit(solution)/shard_map/bhts,bthe->bshe/dot_general | solution.py:74
  123.6 8.1 %all-to-all-done.1 = f32[2,32,2048]{2,0,1:T(2,128)} async-done(((f32[2,32,2048]{2,0,1:T(2,128)}), f32[2,32,2048]{2,0,1:T(2,128)}, u32[]{:S(2)}, u32[]{:S(2)}) %all-to-all-start.1) | async-done | bytes 524320 | tf_op jit(solution)/shard_map/all_to_all | solution.py:40
  131.7 2.5 %fusion.35 = (f32[1,32,2048]{2,0,1:T(1,128)S(1)}, f32[1,32,2048]{2,0,1:T(1,128)}) fusion(f32[2,32,2048]{2,0,1:T(2,128)} %all-to-all-done.1), kind=kLoop, calls=%fused_computation.45 | loop fusion | bytes 1048576 | tf_op jit(solution)/shard_map/slice | solution.py:45
  134.3 3.0 %fusion.10 = bf16[4,256,4,128]{1,3,2,0:T(8,128)(2,1)} fusion(f32[4,4,128,256]{3,2,1,0:T(8,128)} %fusion.6, bf16[4,256,4,128]{3,2,1,0:T(4,128)(2,1)S(1)} %bitcast.49, f32[3,4,128,128]{2,3,1,0:T(8,128)S(1)} %copy-done.3, f32[4,128,128]{1,2,0:T(8,128)S(1)} %copy.93), kind=kOutput, calls=%fused_computation.13 | convolution fusion | flops 136314880 | bytes 5242880 | tf_op jit(solution)/shard_map/bshd,bhde->bshe/dot_general | solution.py:77
  137.3 2.4 %copy.102 = bf16[4,256,4,128]{3,1,0,2:T(8,128)(2,1)} copy(bf16[4,256,4,128]{1,3,2,0:T(8,128)(2,1)} %fusion.10) | data formatting | bytes 2097152 | tf_op jit(solution)/shard_map/convert_element_type | solution.py:84
  139.7 3.1 %copy.105 = bf16[1024,4,128]{2,1,0:T(4,128)(2,1)} copy(bf16[1024,4,128]{2,0,1:T(8,128)(2,1)} %bitcast.60) | data formatting | bytes 2097152
  143.5 1.8 %copy.104 = bf16[1024,4,128]{2,1,0:T(4,128)(2,1)} copy(bf16[1024,4,128]{2,0,1:T(8,128)(2,1)S(1)} %bitcast.61) | data formatting | bytes 2097152
  146.4 1.8 %copy.103 = bf16[1024,4,128]{2,1,0:T(4,128)(2,1)} copy(bf16[1024,4,128]{2,0,1:T(8,128)(2,1)S(1)} %bitcast.62) | data formatting | bytes 2097152
  (47 shorter events, 6.4 us)
Async XLA Ops:
  7.2 57.6 %all-gather.2.cloned.1.call-start = ((), (), s32[]{:S(2)}) async-start(), calls=%async_computation.2 | async-start | bytes 9437184 | tf_op jit(solution)/shard_map/all_gather | solution.py:18
  10.0 62.9 %copy-start.4 = (bf16[1024,4,128]{2,1,0:T(4,128)(2,1)S(1)}, bf16[1024,4,128]{2,1,0:T(4,128)(2,1)}, u32[]{:S(2)}) copy-start(bf16[1024,4,128]{2,1,0:T(4,128)(2,1)} %param.5) | copy-start | bytes 3145732
  72.9 1.3 copy-start.7
  76.6 28.3 %all-to-all-start = ((f32[2,32,2048]{2,0,1:T(2,128)}), f32[2,32,2048]{2,0,1:T(2,128)}, u32[]{:S(2)}, u32[]{:S(2)}) async-start(f32[2,32,2048]{2,0,1:T(2,128)} %copy.84), calls=%async_computation | async-start | bytes 1048576 | tf_op jit(solution)/shard_map/all_to_all | solution.py:37
  87.5 1.0 copy-start.9
  89.4 1.5 copy-start.5
  109.3 22.4 %all-to-all-start.1 = ((f32[2,32,2048]{2,0,1:T(2,128)}), f32[2,32,2048]{2,0,1:T(2,128)}, u32[]{:S(2)}, u32[]{:S(2)}) async-start(f32[2,32,2048]{2,0,1:T(2,128)} %copy.87), calls=%async_computation.1 | async-start | bytes 1048576 | tf_op jit(solution)/shard_map/all_to_all | solution.py:40
  114.2 3.4 %copy-start = (bf16[1024,4,128]{2,1,0:T(4,128)(2,1)S(1)}, bf16[1024,4,128]{2,1,0:T(4,128)(2,1)}, u32[]{:S(2)}) copy-start(bf16[1024,4,128]{2,1,0:T(4,128)(2,1)} %param.6) | copy-start | bytes 3145732
  123.6 10.7 %copy-start.3 = (f32[3,4,128,128]{2,3,1,0:T(8,128)S(1)}, f32[3,4,128,128]{2,3,1,0:T(8,128)}, u32[]{:S(2)}) copy-start(f32[3,4,128,128]{2,3,1,0:T(8,128)} %slice.31) | copy-start | bytes 2359300
  137.3 5.5 %copy-start.2 = (f32[4,4,256,128]{3,2,1,0:T(8,128)S(1)}, f32[4,4,256,128]{3,2,1,0:T(8,128)}, u32[]{:S(2)}) copy-start(f32[4,4,256,128]{3,2,1,0:T(8,128)} %fusion.13) | copy-start | bytes 6291460
  139.7 3.1 %copy-start.6 = (bf16[1024,4,128]{2,1,0:T(4,128)(2,1)S(1)}, bf16[1024,4,128]{2,1,0:T(4,128)(2,1)}, u32[]{:S(2)}) copy-start(bf16[1024,4,128]{2,1,0:T(4,128)(2,1)} %param.7) | copy-start | bytes 3145732
  143.3 1.9 %copy-start.1 = (f32[4,4,256,128]{3,2,1,0:T(8,128)S(1)}, f32[4,4,256,128]{3,2,1,0:T(8,128)}, u32[]{:S(2)}) copy-start(f32[4,4,256,128]{3,2,1,0:T(8,128)} %fusion.24) | copy-start | bytes 6291460
  143.3 1.9 %copy-start.8 = (bf16[1024,4,128]{2,0,1:T(8,128)(2,1)S(1)}, bf16[1024,4,128]{2,0,1:T(8,128)(2,1)}, u32[]{:S(2)}) copy-start(bf16[1024,4,128]{2,0,1:T(8,128)(2,1)} %copy-done.7) | copy-start | bytes 3145732
  143.3 2.4 %slice-start = ((f32[4,4,128,128]{3,2,1,0:T(8,128)}), f32[3,4,128,128]{3,2,1,0:T(8,128)S(1)}, s32[]{:S(2)}) async-start(f32[4,4,128,128]{3,2,1,0:T(8,128)} %copy-done.9), calls=%async_computation.3 | async-start | bytes 1572864 | tf_op jit(solution)/shard_map/slice | solution.py:48
  143.4 2.5 %copy-start.10 = (f32[1,32,2048]{2,0,1:T(1,128)S(1)}, f32[1,32,2048]{2,0,1:T(1,128)}, u32[]{:S(2)}) copy-start(f32[1,32,2048]{2,0,1:T(1,128)} %get-tuple-element.13) | copy-start | bytes 786436
Sparse Core Ops, SparseCore 0:
  9.8 54.8 all-gather.1
where the time goes:
time: 156 us; the launch traced here: 155 us
  waiting for transfers between devices  75.5 us (48%)
  matrix products  26.8 us (17%)
  local copies, waits for them, and re-layouts  21.1 us (14%)
  starting transfers between devices  15.1 us (10%)
  between operations  14.3 us (9%)
  other arithmetic  2.3 us (1%)
    all_gather x1, waiting for transfers between devices, body(): lax.all_gather(out_grad, 'head', axis=1, tiled=True)  54.7 us
    all_to_all x1, waiting for transfers between devices, body(): lax.all_to_all(stacked, 'seq', split_axis=1, concat_axis=1, tiled=True)  12 us
    all_to_all x1, starting transfers between devices, body(): lax.all_to_all(stacked, 'seq', split_axis=1, concat_axis=1, tiled=True)  10.1 us
    unnamed x27, local copies, waits for them, and re-layouts  8.39 us
    dot_general x1, matrix products, body(): jnp.einsum('tm,hdm->thd', lax.all_gather(out_grad, 'head', axis=1, tiled=...  8.22 us
    all_to_all x1, waiting for transfers between devices, body(): lax.all_to_all(jnp.stack([forward_sums, reverse_sums]), 'seq', split_axis...  8.12 us
    all_to_all x1, starting transfers between devices, body(): lax.all_to_all(jnp.stack([forward_sums, reverse_sums]), 'seq', split_axis...  4.9 us
    dot_general x1, matrix products, body(): jnp.einsum('bhts,bthe->bshe', qk_scores, grad_blocks, preferred_element_t...  3.89 us
  transfers between devices with their start and end apart: 3, of which 3 were waited for; matrix products, arithmetic and copies ran while one was open for 10% of the time, Pallas kernels for 0%

commit v1 on v0

--- a/solution.py
+++ b/solution.py
@@ -7,17 +7,38 @@
 BLOCK = 256
 
 
+def summed_both_ways(value, axis, dim, contribution):
+    length, index, rows = (lax.axis_size(axis), lax.axis_index(axis), value.shape[dim])
+    right = [(i, (i + 1) % length) for i in range(length)]
+    left = [(i, (i - 1) % length) for i in range(length)]
+    half = length // 2
+    from_left = from_right = value
+    total = contribution(value, index * rows)
+    for step in range(1, half + 1):
+        from_left = lax.ppermute(from_left, axis, right)
+        if step < length - half:
+            from_right = lax.ppermute(from_right, axis, left)
+            total = total + contribution(from_right, (index + step) % length * rows)
+        total = total + contribution(from_left, (index - step) % length * rows)
+    return total
+
+
 def body(queries, key_rows, value_rows, out_grad, out_weight):
     tokens = queries.shape[0]
     heads = queries.shape[1]
     depth = queries.shape[2]
     blocks = tokens // BLOCK
     factor = 1.0 / math.sqrt(depth * tokens * lax.axis_size("seq"))
-    attn_grad = jnp.einsum(
-        "tm,hdm->thd",
-        lax.all_gather(out_grad, "head", axis=1, tiled=True),
-        out_weight,
-        preferred_element_type=jnp.float32,
+    attn_grad = summed_both_ways(
+        out_grad,
+        "head",
+        1,
+        lambda own_block, offset: jnp.einsum(
+            "tm,hdm->thd",
+            own_block,
+            lax.dynamic_slice_in_dim(out_weight, offset, own_block.shape[1], axis=2),
+            preferred_element_type=jnp.float32,
+        ),
     ).astype(jnp.bfloat16)
     layout = (blocks, BLOCK, heads, depth)
     query_blocks = queries.reshape(layout)

time: 156 us -> 138 us (0.88)
  the two profiles are of different devices: /device:TPU:32 before, /device:TPU:38 now
where the time goes in v1:
time: 138 us; the launch traced here: 137 us
  waiting for transfers between devices  53.6 us (39%)
  matrix products  32.8 us (24%)
  local copies, waits for them, and re-layouts  23.7 us (17%)
  starting transfers between devices  22.5 us (16%)
  other arithmetic  3.33 us (2%)
    ppermute x4, waiting for transfers between devices, summed_both_ways(): from_left = lax.ppermute(from_left, axis, right)  35.2 us
    dot_general x8, matrix products, body(): jnp.einsum('tm,hdm->thd', own_block, lax.dynamic_slice_in_dim(out_weight,...  12.6 us
    all_to_all x1, starting transfers between devices, body(): lax.all_to_all(stacked, 'seq', split_axis=1, concat_axis=1, tiled=True)  11.4 us
    all_to_all x1, waiting for transfers between devices, body(): lax.all_to_all(jnp.stack([forward_sums, reverse_sums]), 'seq', split_axis...  8.28 us
    all_to_all x1, waiting for transfers between devices, body(): lax.all_to_all(stacked, 'seq', split_axis=1, concat_axis=1, tiled=True)  8.18 us
    unnamed x31, local copies, waits for them, and re-layouts  7.87 us
    all_to_all x1, starting transfers between devices, body(): lax.all_to_all(jnp.stack([forward_sums, reverse_sums]), 'seq', split_axis...  5.36 us
    ppermute x3, starting transfers between devices, summed_both_ways(): from_right = lax.ppermute(from_right, axis, left)  5.32 us
  transfers between devices with their start and end apart: 9, of which 7 were waited for; matrix products, arithmetic and copies ran while one was open for 24% of the time, Pallas kernels for 0%

profile of v1, /device:TPU:38, one launch (start us, length us, event | category | flops | bytes accessed | tf_op | source)
XLA Modules:
  0.0 137.0 jit_solution(13262865409520311876)
XLA Ops:
  2.4 12.7 %collective-permute-done.1 = bf16[1024,512]{1,0:T(8,128)(2,1)S(1)} collective-permute-done((bf16[1024,512]{1,0:T(8,128)(2,1)}, bf16[1024,512]{1,0:T(8,128)(2,1)S(1)}, u32[]{:S(2)}, u32[]{:S(2)}) %collective-permute-start.1) | collective-permute-done | bytes 1048608 | tf_op jit(solution)/shard_map/ppermute | solution.py:18
  15.1 1.8 %collective-permute-start.2 = (bf16[1024,512]{1,0:T(8,128)(2,1)}, bf16[1024,512]{1,0:T(8,128)(2,1)}, u32[]{:S(2)}, u32[]{:S(2)}) collective-permute-start(bf16[1024,512]{1,0:T(8,128)(2,1)} %collective-permute-done), channel_id=1, source_target_pairs={{0,7},{1,0},{2,1},{3,2},{4,3},{5,4},{6,5},{7,6},{8,15},{9,8},{10,9... | collective-permute-start | bytes 3145736 | tf_op jit(solution)/shard_map/ppermute | solution.py:20
  16.9 12.4 %collective-permute-done.3 = bf16[1024,512]{1,0:T(8,128)(2,1)S(1)} collective-permute-done((bf16[1024,512]{1,0:T(8,128)(2,1)S(1)}, bf16[1024,512]{1,0:T(8,128)(2,1)S(1)}, u32[]{:S(2)}, u32[]{:S(2)}) %collective-permute-start.3) | collective-permute-done | bytes 1048608 | tf_op jit(solution)/shard_map/ppermute | solution.py:18
  29.3 2.1 %fusion.64 = (f32[4,128,128]{2,1,0:T(8,128)S(1)}, f32[4,4,128,128]{3,2,1,0:T(8,128)S(1)}) fusion(bf16[4,256,4,128]{3,2,1,0:T(4,128)(2,1)} %bitcast.86, bf16[4,256,4,128]{3,2,1,0:T(4,128)(2,1)} %bitcast.76), kind=kOutput, calls=%fused_computation.77 | convolution fusion | flops 134414336 | bytes 3407872 | tf_op jit(solution)/shard_map/bthd,bthe->bhde/dot_general | solution.py:48
  32.3 1.9 %fusion.21 = f32[4,128,1024]{2,1,0:T(8,128)S(1)} fusion(bf16[1024,512]{1,0:T(8,128)(2,1)S(1)} %copy-done.11, bf16[4,128,4096]{2,1,0:T(8,128)(2,1)} %param.9, s32[]{:T(128)S(6)} %select_n.64), kind=kOutput, calls=%fused_computation.28 | convolution fusion | flops 536870912 | bytes 3670020 | tf_op jit(solution)/shard_map/tm,hdm->thd/dot_general | solution.py:36
  34.2 2.1 %fusion.17 = f32[4,128,1024]{2,1,0:T(8,128)S(1)} fusion(bf16[1024,512]{1,0:T(8,128)(2,1)} %copy-done.12, bf16[4,128,4096]{2,1,0:T(8,128)(2,1)} %param.9, s32[]{:T(128)S(6)} %select_n.68), kind=kOutput, calls=%fused_computation.24 | convolution fusion | flops 536870912 | bytes 3670020 | tf_op jit(solution)/shard_map/tm,hdm->thd/dot_general | solution.py:36
  38.1 2.0 %fusion.19 = f32[4,128,1024]{2,1,0:T(8,128)S(1)} fusion(bf16[1024,512]{1,0:T(8,128)(2,1)} %collective-permute-done, bf16[4,128,4096]{2,1,0:T(8,128)(2,1)S(1)} %copy-done.8, s32[]{:T(128)S(6)} %select_n.66), kind=kOutput, calls=%fused_computation.26 | convolution fusion | flops 536870912 | bytes 3670020 | tf_op jit(solution)/shard_map/tm,hdm->thd/dot_general | solution.py:36
  40.1 3.5 %collective-permute-done.5 = bf16[1024,512]{1,0:T(8,128)(2,1)} collective-permute-done((bf16[1024,512]{1,0:T(8,128)(2,1)S(1)}, bf16[1024,512]{1,0:T(8,128)(2,1)}, u32[]{:S(2)}, u32[]{:S(2)}) %collective-permute-start.5) | collective-permute-done | bytes 1048608 | tf_op jit(solution)/shard_map/ppermute | solution.py:18
  44.8 2.0 %fusion.15 = f32[4,128,1024]{2,1,0:T(8,128)S(1)} fusion(bf16[1024,512]{1,0:T(8,128)(2,1)} %collective-permute-done.2, bf16[4,128,4096]{2,1,0:T(8,128)(2,1)S(1)} %copy-done.8, s32[]{:T(128)S(6)} %select_n.70), kind=kOutput, calls=%fused_computation.22 | convolution fusion | flops 536870912 | bytes 3670020 | tf_op jit(solution)/shard_map/tm,hdm->thd/dot_general | solution.py:36
  46.8 2.0 %fusion.9 = f32[4,128,1024]{2,1,0:T(8,128)S(1)} fusion(bf16[1024,512]{1,0:T(8,128)(2,1)} %collective-permute-done.5, bf16[4,128,4096]{2,1,0:T(8,128)(2,1)S(1)} %copy-done.8, s32[]{:T(128)S(6)} %select_n.76), kind=kOutput, calls=%fused_computation.16 | convolution fusion | flops 536870912 | bytes 3670020 | tf_op jit(solution)/shard_map/tm,hdm->thd/dot_general | solution.py:36
  48.8 2.0 %collective-permute-done.4 = bf16[1024,512]{1,0:T(8,128)(2,1)S(1)} collective-permute-done((bf16[1024,512]{1,0:T(8,128)(2,1)}, bf16[1024,512]{1,0:T(8,128)(2,1)S(1)}, u32[]{:S(2)}, u32[]{:S(2)}) %collective-permute-start.4) | collective-permute-done | bytes 1048608 | tf_op jit(solution)/shard_map/ppermute | solution.py:20
  51.5 6.6 %collective-permute-done.6 = bf16[1024,512]{1,0:T(8,128)(2,1)S(1)} collective-permute-done((bf16[1024,512]{1,0:T(8,128)(2,1)}, bf16[1024,512]{1,0:T(8,128)(2,1)S(1)}, u32[]{:S(2)}, u32[]{:S(2)}) %collective-permute-start.6) | collective-permute-done | bytes 1048608 | tf_op jit(solution)/shard_map/ppermute | solution.py:18
  64.5 11.4 %all-to-all-start = ((f32[2,32,2048]{2,0,1:T(2,128)}), f32[2,32,2048]{2,0,1:T(2,128)}, u32[]{:S(2)}, u32[]{:S(2)}) async-start(f32[2,32,2048]{2,0,1:T(2,128)} %copy.84), calls=%async_computation | async-start | bytes 1048576 | tf_op jit(solution)/shard_map/all_to_all | solution.py:58
  80.2 2.4 %copy.76 = bf16[4,256,4,128]{3,1,2,0:T(8,128)(2,1)} copy(bf16[4,256,4,128]{1,0,3,2:T(4,128)(2,1)} %reshape.40) | data formatting | bytes 2097152 | tf_op jit(solution)/shard_map/reshape | solution.py:47
  82.6 3.2 %select_convert_fusion.1 = bf16[4,4,256,256]{3,2,1,0:T(8,128)(2,1)} fusion(bf16[4,256,4,128]{3,1,2,0:T(8,128)(2,1)} %copy.76, pred[256,256]{1,0:T(8,128)(4,1)S(1)} %iota_compare_fusion, bf16[4,256,4,128]{3,2,1,0:T(4,128)(2,1)S(1)} %bitcast.87), kind=kOutput, calls=%fused_computation.1 | convolution fusion | flops 270532608 | bytes 4259840 | tf_op jit(solution)/shard_map/bthd,bshd->bhts/dot_general | solution.py:79
  85.9 8.2 %all-to-all-done = f32[2,32,2048]{2,0,1:T(2,128)} async-done(((f32[2,32,2048]{2,0,1:T(2,128)}), f32[2,32,2048]{2,0,1:T(2,128)}, u32[]{:S(2)}, u32[]{:S(2)}) %all-to-all-start) | async-done | bytes 524320 | tf_op jit(solution)/shard_map/all_to_all | solution.py:58
  98.5 5.4 %all-to-all-start.1 = ((f32[2,32,2048]{2,0,1:T(2,128)}), f32[2,32,2048]{2,0,1:T(2,128)S(1)}, u32[]{:S(2)}, u32[]{:S(2)}) async-start(f32[2,32,2048]{2,0,1:T(2,128)} %copy.87), calls=%async_computation.1 | async-start | bytes 1048576 | tf_op jit(solution)/shard_map/all_to_all | solution.py:61
  103.9 4.1 %fusion.27 = f32[4,4,256,128]{3,2,1,0:T(8,128)} fusion(bf16[4,4,256,256]{3,2,1,0:T(8,128)(2,1)} %select_convert_fusion.1, bf16[4,256,4,128]{3,2,1,0:T(4,128)(2,1)} %bitcast.83), kind=kOutput, calls=%fused_computation.35 | convolution fusion | flops 268435456 | bytes 5242880 | tf_op jit(solution)/shard_map/bhts,bthd->bshd/dot_general | solution.py:89
  108.0 2.0 %fusion.38 = f32[4,4,256,128]{3,2,1,0:T(8,128)} fusion(bf16[4,4,256,256]{3,2,1,0:T(8,128)(2,1)S(1)} %copy-done.1, bf16[4,256,4,128]{3,2,1,0:T(4,128)(2,1)S(1)} %bitcast.77), kind=kOutput, calls=%fused_computation.45 | convolution fusion | flops 268435456 | bytes 5242880 | tf_op jit(solution)/shard_map/bhts,bshd->bthd/dot_general | solution.py:83
  110.0 3.6 %fusion.4 = f32[4,4,128,256]{3,2,1,0:T(8,128)} fusion(pred[256,256]{1,0:T(8,128)(4,1)S(1)} %iota_compare_fusion, bf16[4,16,4,8,256]{4,3,2,1,0:T(8,128)(2,1)S(1)} %bitcast.82, bf16[4,256,4,128]{3,2,1,0:T(4,128)(2,1)} %bitcast.84, bf16[4,256,4,128]{3,2,1,0:T(4,128)(2,1)S(1)} %bitcast.78), kind=kOutput, calls=%fused_computation.10 | convolution fusion | flops 538968064 | bytes 5308416 | tf_op jit(solution)/shard_map/bhts,bthe->bshe/dot_general | solution.py:95
  113.6 8.3 %all-to-all-done.1 = f32[2,32,2048]{2,0,1:T(2,128)S(1)} async-done(((f32[2,32,2048]{2,0,1:T(2,128)}), f32[2,32,2048]{2,0,1:T(2,128)S(1)}, u32[]{:S(2)}, u32[]{:S(2)}) %all-to-all-start.1) | async-done | bytes 524320 | tf_op jit(solution)/shard_map/all_to_all | solution.py:61
  123.1 3.0 %fusion.5 = bf16[4,256,4,128]{1,3,2,0:T(8,128)(2,1)} fusion(f32[4,4,128,256]{3,2,1,0:T(8,128)} %fusion.4, bf16[4,256,4,128]{3,2,1,0:T(4,128)(2,1)S(1)} %bitcast.79, f32[3,4,128,128]{2,3,1,0:T(8,128)S(1)} %slice.31, f32[4,128,128]{1,2,0:T(8,128)S(1)} %copy.93), kind=kOutput, calls=%fused_computation.11 | convolution fusion | flops 136314880 | bytes 5242880 | tf_op jit(solution)/shard_map/bshd,bhde->bshe/dot_general | solution.py:98
  126.1 2.4 %copy.102 = bf16[4,256,4,128]{3,1,0,2:T(8,128)(2,1)} copy(bf16[4,256,4,128]{1,3,2,0:T(8,128)(2,1)} %fusion.5) | data formatting | bytes 2097152 | tf_op jit(solution)/shard_map/convert_element_type | solution.py:105
  128.6 3.1 %copy.105 = bf16[1024,4,128]{2,1,0:T(4,128)(2,1)} copy(bf16[1024,4,128]{2,0,1:T(8,128)(2,1)} %bitcast.89) | data formatting | bytes 2097152
  (71 shorter events, 27.7 us)
Async XLA Ops:
  0.6 31.7 %copy-start.11 = (bf16[1024,512]{1,0:T(8,128)(2,1)S(1)}, bf16[1024,512]{1,0:T(8,128)(2,1)}, u32[]{:S(2)}) copy-start(bf16[1024,512]{1,0:T(8,128)(2,1)} %param.8) | copy-start | bytes 3145732
  0.6 14.4 %collective-permute-start.1 = (bf16[1024,512]{1,0:T(8,128)(2,1)}, bf16[1024,512]{1,0:T(8,128)(2,1)S(1)}, u32[]{:S(2)}, u32[]{:S(2)}) collective-permute-start(bf16[1024,512]{1,0:T(8,128)(2,1)} %param.8), channel_id=1, source_target_pairs={{0,1},{1,2},{2,3},{3,4},{4,5},{5,6},{6,7},{7,0},{8,9},{9,10},{10,1... | collective-permute-start | bytes 3145736 | tf_op jit(solution)/shard_map/ppermute | solution.py:18
  0.7 14.4 %collective-permute-start = (bf16[1024,512]{1,0:T(8,128)(2,1)}, bf16[1024,512]{1,0:T(8,128)(2,1)}, u32[]{:S(2)}, u32[]{:S(2)}) collective-permute-start(bf16[1024,512]{1,0:T(8,128)(2,1)} %param.8), channel_id=1, source_target_pairs={{0,7},{1,0},{2,1},{3,2},{4,3},{5,4},{6,5},{7,6},{8,15},{9,8},{10,9... | collective-permute-start | bytes 3145736 | tf_op jit(solution)/shard_map/ppermute | solution.py:20
  15.1 14.2 %copy-start.12 = (bf16[1024,512]{1,0:T(8,128)(2,1)}, bf16[1024,512]{1,0:T(8,128)(2,1)S(1)}, u32[]{:S(2)}) copy-start(bf16[1024,512]{1,0:T(8,128)(2,1)S(1)} %collective-permute-done.1) | copy-start | bytes 3145732
  15.1 14.2 %collective-permute-start.3 = (bf16[1024,512]{1,0:T(8,128)(2,1)S(1)}, bf16[1024,512]{1,0:T(8,128)(2,1)S(1)}, u32[]{:S(2)}, u32[]{:S(2)}) collective-permute-start(bf16[1024,512]{1,0:T(8,128)(2,1)S(1)} %collective-permute-done.1), channel_id=1, source_target_pairs={{0,1},{1,2},{2,3},{3,4},{4,5},{5,6},{6,7},{7,0},{8,9},{9,10},{10,1... | collective-permute-start | bytes 3145736 | tf_op jit(solution)/shard_map/ppermute | solution.py:18
  15.1 21.3 %collective-permute-start.2 = (bf16[1024,512]{1,0:T(8,128)(2,1)}, bf16[1024,512]{1,0:T(8,128)(2,1)}, u32[]{:S(2)}, u32[]{:S(2)}) collective-permute-start(bf16[1024,512]{1,0:T(8,128)(2,1)} %collective-permute-done), channel_id=1, source_target_pairs={{0,7},{1,0},{2,1},{3,2},{4,3},{5,4},{6,5},{7,6},{8,15},{9,8},{10,9... | collective-permute-start | bytes 3145736 | tf_op jit(solution)/shard_map/ppermute | solution.py:20
  29.3 14.3 %collective-permute-start.5 = (bf16[1024,512]{1,0:T(8,128)(2,1)S(1)}, bf16[1024,512]{1,0:T(8,128)(2,1)}, u32[]{:S(2)}, u32[]{:S(2)}) collective-permute-start(bf16[1024,512]{1,0:T(8,128)(2,1)S(1)} %collective-permute-done.3), channel_id=1, source_target_pairs={{0,1},{1,2},{2,3},{3,4},{4,5},{5,6},{6,7},{7,0},{8,9},{9,10},{10,1... | collective-permute-start | bytes 3145736 | tf_op jit(solution)/shard_map/ppermute | solution.py:18
  32.3 5.8 %copy-start.8 = (bf16[4,128,4096]{2,1,0:T(8,128)(2,1)S(1)}, bf16[4,128,4096]{2,1,0:T(8,128)(2,1)}, u32[]{:S(2)}) copy-start(bf16[4,128,4096]{2,1,0:T(8,128)(2,1)} %param.9) | copy-start | bytes 12582916
  36.4 14.4 %collective-permute-start.4 = (bf16[1024,512]{1,0:T(8,128)(2,1)}, bf16[1024,512]{1,0:T(8,128)(2,1)S(1)}, u32[]{:S(2)}, u32[]{:S(2)}) collective-permute-start(bf16[1024,512]{1,0:T(8,128)(2,1)} %collective-permute-done.2), channel_id=1, source_target_pairs={{0,7},{1,0},{2,1},{3,2},{4,3},{5,4},{6,5},{7,6},{8,15},{9,8},{10,9... | collective-permute-start | bytes 3145736 | tf_op jit(solution)/shard_map/ppermute | solution.py:20
  43.6 14.4 %collective-permute-start.6 = (bf16[1024,512]{1,0:T(8,128)(2,1)}, bf16[1024,512]{1,0:T(8,128)(2,1)S(1)}, u32[]{:S(2)}, u32[]{:S(2)}) collective-permute-start(bf16[1024,512]{1,0:T(8,128)(2,1)} %collective-permute-done.5), channel_id=1, source_target_pairs={{0,1},{1,2},{2,3},{3,4},{4,5},{5,6},{6,7},{7,0},{8,9},{9,10},{10,1... | collective-permute-start | bytes 3145736 | tf_op jit(solution)/shard_map/ppermute | solution.py:18
  51.5 7.7 %copy-start.4 = (bf16[1024,4,128]{2,1,0:T(4,128)(2,1)S(1)}, bf16[1024,4,128]{2,1,0:T(4,128)(2,1)}, u32[]{:S(2)}) copy-start(bf16[1024,4,128]{2,1,0:T(4,128)(2,1)} %param.5) | copy-start | bytes 3145732
  64.5 29.6 %all-to-all-start = ((f32[2,32,2048]{2,0,1:T(2,128)}), f32[2,32,2048]{2,0,1:T(2,128)}, u32[]{:S(2)}, u32[]{:S(2)}) async-start(f32[2,32,2048]{2,0,1:T(2,128)} %copy.84), calls=%async_computation | async-start | bytes 1048576 | tf_op jit(solution)/shard_map/all_to_all | solution.py:58
  76.7 1.0 copy-start.9
  78.6 4.0 %copy-start.5 = (bf16[1024,4,128]{2,1,0:T(4,128)(2,1)S(1)}, bf16[1024,4,128]{2,1,0:T(4,128)(2,1)}, u32[]{:S(2)}) copy-start(bf16[1024,4,128]{2,1,0:T(4,128)(2,1)} %param.7) | copy-start | bytes 3145732
  98.5 23.4 %all-to-all-start.1 = ((f32[2,32,2048]{2,0,1:T(2,128)}), f32[2,32,2048]{2,0,1:T(2,128)S(1)}, u32[]{:S(2)}, u32[]{:S(2)}) async-start(f32[2,32,2048]{2,0,1:T(2,128)} %copy.87), calls=%async_computation.1 | async-start | bytes 1048576 | tf_op jit(solution)/shard_map/all_to_all | solution.py:61
  103.9 4.1 %copy-start = (bf16[1024,4,128]{2,1,0:T(4,128)(2,1)S(1)}, bf16[1024,4,128]{2,1,0:T(4,128)(2,1)}, u32[]{:S(2)}) copy-start(bf16[1024,4,128]{2,1,0:T(4,128)(2,1)} %param.6) | copy-start | bytes 3145732
  103.9 4.1 %copy-start.1 = (bf16[4,4,256,256]{3,2,1,0:T(8,128)(2,1)S(1)}, bf16[4,4,256,256]{3,2,1,0:T(8,128)(2,1)}, u32[]{:S(2)}) copy-start(bf16[4,4,256,256]{3,2,1,0:T(8,128)(2,1)} %select_convert_fusion.1) | copy-start | bytes 6291460
  126.1 5.5 %copy-start.3 = (f32[4,4,256,128]{3,2,1,0:T(8,128)S(1)}, f32[4,4,256,128]{3,2,1,0:T(8,128)}, u32[]{:S(2)}) copy-start(f32[4,4,256,128]{3,2,1,0:T(8,128)} %fusion.27) | copy-start | bytes 6291460
  128.6 3.1 %copy-start.6 = (bf16[1024,4,128]{2,1,0:T(4,128)(2,1)S(1)}, bf16[1024,4,128]{2,1,0:T(4,128)(2,1)}, u32[]{:S(2)}) copy-start(bf16[1024,4,128]{2,1,0:T(4,128)(2,1)} %param.7) | copy-start | bytes 3145732
  132.2 1.9 %copy-start.2 = (f32[4,4,256,128]{3,2,1,0:T(8,128)S(1)}, f32[4,4,256,128]{3,2,1,0:T(8,128)}, u32[]{:S(2)}) copy-start(f32[4,4,256,128]{3,2,1,0:T(8,128)} %fusion.38) | copy-start | bytes 6291460
  132.2 1.9 %copy-start.7 = (bf16[4,256,4,128]{3,1,2,0:T(8,128)(2,1)S(1)}, bf16[4,256,4,128]{3,1,2,0:T(8,128)(2,1)}, u32[]{:S(2)}) copy-start(bf16[4,256,4,128]{3,1,2,0:T(8,128)(2,1)} %copy.76) | copy-start | bytes 3145732
  132.2 2.4 %slice-start = ((f32[4,4,128,128]{3,2,1,0:T(8,128)}), f32[3,4,128,128]{3,2,1,0:T(8,128)S(1)}, s32[]{:S(2)}) async-start(f32[4,4,128,128]{3,2,1,0:T(8,128)} %copy-done.9), calls=%async_computation.2 | async-start | bytes 1572864 | tf_op jit(solution)/shard_map/slice | solution.py:69
  132.2 2.5 %copy-start.10 = (f32[1,32,2048]{2,0,1:T(1,128)S(1)}, f32[1,32,2048]{2,0,1:T(1,128)}, u32[]{:S(2)}) copy-start(f32[1,32,2048]{2,0,1:T(1,128)} %get-tuple-element.13) | copy-start | bytes 786436
